TPU v7x, 256 devices: a whole 4x4x8 slice. The times are simulated.
256 devices in a mesh: expert: 64 (over y_lo, x, z), tensor: 4 (over y_hi, core).
Axes of the slice: x: 4, y: 4 (y_hi: 2, y_lo: 2; y = y_hi * 2 + y_lo), z: 8, core: 2. Of those that a mesh axis runs over, the one named last changes fastest.
Arguments:
- tokens: bfloat16 [8192, 4096], P('expert', 'tensor'), may hold values from -6 to 6
- residual_grad: bfloat16 [8192, 4096], P('expert', 'tensor'), may hold values from -6 to 6
- dense_hidden: bfloat16 [8192, 2560], P('expert', 'tensor'), may hold values from -6 to 6
- dense_gate: bfloat16 [4096, 2560], P('expert', 'tensor'), may hold values from -0.09375 to 0.09375
- dense_up: bfloat16 [4096, 2560], P('expert', 'tensor'), may hold values from -0.09375 to 0.09375
- expert_gate: bfloat16 [64, 4096, 2560], P('expert', None, 'tensor'), may hold values from -0.09375 to 0.09375
- expert_up: bfloat16 [64, 4096, 2560], P('expert', None, 'tensor'), may hold values from -0.09375 to 0.09375
- expert_hidden: bfloat16 [64, 320, 2560], P('expert', None, 'tensor'), may hold values from -6 to 6
- expert_ids: int32 [8192, 2], P('expert'), may hold values from 0 to 63, as said below
- slot_index: int32 [8192, 2], P('expert'), may hold values from 0 to 5, as said below
- kept_mask: int32 [8192, 2], P('expert'), may hold values from 0 to 1, as said below
- gate_weights: float32 [8192, 2], P('expert'), may hold values from 0.2 to 1
Outputs:
- input_grad: bfloat16 [8192, 4096], P('expert', 'tensor')
Inputs may be any that keep to these rules, and one draw needn't show every extreme that they name: `expert_ids`: the two experts of a token differ. In every group of 128 tokens (the tokens of one index of expert) some expert is named by more than 5 assignments. `slot_index`: within a group of 128 tokens, the assignments to one expert are counted in the order of all first choices in token order, then all second choices in token order; a kept assignment's slot is the number of assignments to its expert before it, and a dropped one has 5. `kept_mask`: 1 exactly where the count in that order is below 5.
All inputs are finite; a program needn't handle non-finite values.
Results may differ from a plain program's by a relative error of at most 0.014.
Values may be sent and summed in bfloat16 or wider, within the bound.
A program may use at most 128 MiB of HBM per device.

v0:
```python
import jax
import jax.numpy as jnp
from jax import lax
from jax.sharding import PartitionSpec as P


def activation_back(pre_gate, pre_up, hidden_grad):
    upstream = hidden_grad.astype(jnp.float32)
    sigmoid_gate = jax.nn.sigmoid(pre_gate)
    gate_back = (upstream * pre_up * sigmoid_gate * (1.0 + pre_gate * (1.0 - sigmoid_gate))).astype(
        jnp.bfloat16
    )
    up_back = (upstream * pre_gate * sigmoid_gate).astype(jnp.bfloat16)
    return (gate_back, up_back)


def project_back(gate_back, up_back, gate_matrix, up_matrix):
    first_term = jnp.einsum("tf,df->td", gate_back, gate_matrix, preferred_element_type=jnp.float32)
    return first_term + jnp.einsum(
        "tf,df->td", up_back, up_matrix, preferred_element_type=jnp.float32
    )


def swiglu_back(inputs, gate_matrix, up_matrix, hidden_grad):
    pre_gate = jnp.dot(inputs, gate_matrix, preferred_element_type=jnp.float32)
    pre_up = jnp.dot(inputs, up_matrix, preferred_element_type=jnp.float32)
    gate_back, up_back = activation_back(pre_gate, pre_up, hidden_grad)
    return project_back(gate_back, up_back, gate_matrix, up_matrix)


def pack_slots(inputs, flat_slot, slots_total, groups):
    spread = jnp.broadcast_to(inputs[:, None, :], (inputs.shape[0], 2, inputs.shape[1])).reshape(
        -1, inputs.shape[1]
    )
    buffer = (
        jnp.zeros((slots_total, inputs.shape[1]), inputs.dtype)
        .at[flat_slot.reshape(-1)]
        .add(spread, mode="drop")
    )
    return buffer.reshape(groups, slots_total // groups, inputs.shape[1])


def combine(returned, flat_slot, weights):
    buffer = returned.reshape(-1, returned.shape[-1])
    picked = buffer[jnp.minimum(flat_slot, buffer.shape[0] - 1)]
    return jnp.sum(picked * weights[:, :, None], axis=1)


def body(
    tokens,
    residual_grad,
    dense_hidden,
    dense_gate,
    dense_up,
    expert_gate,
    expert_up,
    expert_hidden,
    expert_ids,
    slot_index,
    kept_mask,
    gate_weights,
):
    groups = lax.axis_size("expert")
    capacity = expert_hidden.shape[1] // groups
    whole_rows = lax.all_gather(tokens, "tensor", axis=1, tiled=True)
    full_gate, full_up = (
        lax.all_gather(dense_gate, "expert", axis=0, tiled=True),
        lax.all_gather(dense_up, "expert", axis=0, tiled=True),
    )
    dense_part = swiglu_back(whole_rows, full_gate, full_up, dense_hidden)
    take_mask = (kept_mask == 1) & (slot_index < capacity)
    flat_slot = jnp.where(take_mask, expert_ids * capacity + slot_index, groups * capacity)
    weights = jnp.where(take_mask, gate_weights, 0.0)
    received = lax.all_to_all(
        pack_slots(whole_rows, flat_slot, groups * capacity, groups),
        "expert",
        split_axis=0,
        concat_axis=0,
        tiled=True,
    )
    expert_in = received.reshape(groups * capacity, received.shape[2])
    expert_part = swiglu_back(expert_in, expert_gate[0], expert_up[0], expert_hidden[0])
    returned = lax.all_to_all(
        expert_part.reshape(groups, capacity, expert_part.shape[1]).astype(jnp.bfloat16),
        "expert",
        split_axis=0,
        concat_axis=0,
        tiled=True,
    ).astype(jnp.float32)
    together = dense_part + combine(returned, flat_slot, weights)
    summed = lax.psum_scatter(
        together.astype(jnp.bfloat16), "tensor", scatter_dimension=1, tiled=True
    ).astype(jnp.float32)
    return (residual_grad.astype(jnp.float32) + summed).astype(jnp.bfloat16)


def solution(mesh):
    placed = (
        P("expert", "tensor"),
        P("expert", "tensor"),
        P("expert", "tensor"),
        P("expert", "tensor"),
        P("expert", "tensor"),
        P("expert", None, "tensor"),
        P("expert", None, "tensor"),
        P("expert", None, "tensor"),
        P("expert", None),
        P("expert", None),
        P("expert", None),
        P("expert", None),
    )
    return jax.shard_map(
        body, mesh=mesh, in_specs=placed, out_specs=P("expert", "tensor"), check_vma=False
    )
```

profile of v0, /device:TPU:1, one launch (start us, length us, event | category | flops | bytes accessed | tf_op | source)
XLA Modules:
  0.0 773.1 jit_solution(3100299195218039832)
XLA Ops:
  6.5 0.0 all-gather.4.cloned.1.call-start
  6.5 0.7 all-gather.4.cloned.1.call-update
  7.3 0.0 all-gather.8.cloned.1.call-start
  7.3 0.7 all-gather.8.cloned.1.call-update
  8.0 0.7 compare_select_fusion.1
  8.7 0.1 copy.14
  8.8 0.1 reshape.52
  9.0 27.8 %all-gather.4.cloned.1.call-done = bf16[128,4096]{1,0:T(8,128)(2,1)} async-done(((bf16[128,1024]{1,0:T(8,128)(2,1)}), bf16[128,4096]{1,0:T(8,128)(2,1)}) %all-gather.4.cloned.1.call-update) | async-done | bytes 1048592 | tf_op jit(solution)/shard_map/all_gather | solution.py:65
  36.7 3.3 broadcast_in_dim.24
  40.1 2.2 reshape.73
  42.3 8.2 %scatter_custom_fusion = bf16[320,4096]{1,0:T(8,128)(2,1)S(1)} fusion(s32[256]{0:T(256)S(1)} %bitcast.37, bf16[256,4096]{1,0:T(8,128)(2,1)} %reshape.73, bf16[]{:T(256)} %constant.9.clone.1), kind=kCustom, calls=%fused_computation.15 | custom fusion | flops 1048576 | bytes 2621952 | tf_op jit(solution)/shard_map/scatter-add | solution.py:38
  50.5 2.9 reshape.54
  53.4 10.4 %all-to-all-start = ((bf16[64,5,4096]{2,1,0:T(8,128)(2,1)}), bf16[64,5,4096]{2,1,0:T(8,128)(2,1)}, u32[]{:S(2)}, u32[]{:S(2)}) async-start(bf16[64,5,4096]{2,1,0:T(8,128)(2,1)} %reshape.54), calls=%async_computation | async-start | bytes 8388608 | tf_op jit(solution)/shard_map/all_to_all | solution.py:74
  63.8 0.2 all-gather.6.cloned.1.call-start
  64.1 0.5 all-gather.6.cloned.1.call-update
  64.6 109.0 %all-to-all-done = bf16[64,5,4096]{2,1,0:T(8,128)(2,1)} async-done(((bf16[64,5,4096]{2,1,0:T(8,128)(2,1)}), bf16[64,5,4096]{2,1,0:T(8,128)(2,1)}, u32[]{:S(2)}, u32[]{:S(2)}) %all-to-all-start) | async-done | bytes 2621472 | tf_op jit(solution)/shard_map/all_to_all | solution.py:74
  173.5 3.4 reshape.55
  177.0 0.0 copy-start.6
  177.0 0.0 slice-start
  177.0 0.0 slice-start.2
  177.0 4.8 fusion.3
  181.8 0.0 copy-done.6
  181.9 0.0 slice-start.1
  181.9 0.0 slice-start.3
  181.9 4.9 fusion.21
  186.8 0.0 slice-done
  186.8 0.0 slice-done.1
  186.8 2.2 fusion.1
  189.1 0.0 slice-done.2
  189.1 0.0 slice-done.3
  189.1 2.2 fusion
  191.3 2.9 convert_element_type.49
  194.2 0.0 copy-start.3
  194.2 0.0 copy-start.4
  194.2 0.0 copy-start.5
  194.2 0.0 copy-start
  194.2 12.6 %all-to-all-start.1 = ((bf16[64,5,4096]{2,1,0:T(8,128)(2,1)}), bf16[64,5,4096]{2,1,0:T(8,128)(2,1)}, u32[]{:S(2)}, u32[]{:S(2)}) async-start(bf16[64,5,4096]{2,1,0:T(8,128)(2,1)} %convert_element_type.49), calls=%async_computation.1 | async-start | bytes 8388608 | tf_op jit(solution)/shard_map/all_to_all | solution.py:83
  206.8 0.3 reduce-scatter.2.cloned.1.call-start
  207.1 0.1 copy.15
  207.2 0.1 reshape.63
  207.3 0.0 copy-done.3
  207.3 0.0 copy-done.4
  207.3 0.0 copy-done.5
  207.4 0.1 copy.16
  207.5 150.8 %all-gather.8.cloned.1.call-done = bf16[4096,640]{1,0:T(8,128)(2,1)} async-done(((bf16[64,640]{1,0:T(8,128)(2,1)}), bf16[4096,640]{1,0:T(8,128)(2,1)}) %all-gather.8.cloned.1.call-update) | async-done | bytes 5242896 | tf_op jit(solution)/shard_map/all_gather | solution.py:67
  358.3 0.0 copy-done
  358.3 3.5 fusion.45
  361.8 286.8 %all-gather.6.cloned.1.call-done = bf16[4096,640]{1,0:T(8,128)(2,1)} async-done(((bf16[64,640]{1,0:T(8,128)(2,1)}), bf16[4096,640]{1,0:T(8,128)(2,1)}) %all-gather.6.cloned.1.call-update) | async-done | bytes 5242896 | tf_op jit(solution)/shard_map/all_gather | solution.py:68
  648.6 6.8 fusion.27
  655.3 0.0 all-to-all-done.1
  655.3 5.3 reshape.60
  660.7 8.3 %gather_fusion = f32[256,4096]{1,0:T(8,128)} fusion(f32[320,4096]{1,0:T(8,128)} %reshape.60, s32[1024]{0:T(1024)S(1)} %pad_clamp_fusion), kind=kCustom, calls=%fused_computation | custom fusion | bytes 8389632 | tf_op jit(solution)/shard_map/gather | solution.py:45
  668.9 5.9 reshape.62
  674.8 0.0 copy-start.1
  674.8 8.7 %multiply_reduce_fusion = f32[128,4096]{1,0:T(8,128)S(1)} fusion(f32[128,2,4096]{2,1,0:T(2,128)} %reshape.62, f32[128,2]{1,0:T(8,128)S(1)} %copy.16), kind=kLoop, calls=%fused_computation.14 | loop fusion | flops 1572864 | bytes 6292480 | tf_op jit(solution)/shard_map/reduce_sum | solution.py:46
  683.6 0.0 copy-done.1
  683.6 0.0 copy-start.2
  683.6 5.4 fusion.9
  689.0 0.0 reduce-scatter.2.cloned.1.call-update
  689.0 75.9 %reduce-scatter.2.cloned.1.call-done = bf16[128,1024]{1,0:T(8,128)(2,1)} async-done(((bf16[128,4096]{1,0:T(8,128)(2,1)}), bf16[128,1024]{1,0:T(8,128)(2,1)}) %reduce-scatter.2.cloned.1.call-update) | async-done | bytes 262160 | tf_op jit(solution)/shard_map/reduce_scatter | solution.py:91
  764.9 0.0 copy-done.2
  764.9 1.7 add_convert_fusion
  (5 shorter events, 0.0 us)
Async XLA Ops:
  6.5 30.2 %all-gather.4.cloned.1.call-start = ((), (), s32[]{:S(2)}) async-start(), calls=%async_computation.3 | async-start | bytes 1310720 | tf_op jit(solution)/shard_map/all_gather | solution.py:65
  7.3 351.0 %all-gather.8.cloned.1.call-start = ((), (), s32[]{:S(2)}) async-start(), calls=%async_computation.5 | async-start | bytes 5324800 | tf_op jit(solution)/shard_map/all_gather | solution.py:67
  53.4 120.2 %all-to-all-start = ((bf16[64,5,4096]{2,1,0:T(8,128)(2,1)}), bf16[64,5,4096]{2,1,0:T(8,128)(2,1)}, u32[]{:S(2)}, u32[]{:S(2)}) async-start(bf16[64,5,4096]{2,1,0:T(8,128)(2,1)} %reshape.54), calls=%async_computation | async-start | bytes 8388608 | tf_op jit(solution)/shard_map/all_to_all | solution.py:74
  63.8 584.7 %all-gather.6.cloned.1.call-start = ((), (), s32[]{:S(2)}) async-start(), calls=%async_computation.4 | async-start | bytes 5324800 | tf_op jit(solution)/shard_map/all_gather | solution.py:68
  177.0 4.9 copy-start.6
  177.0 9.8 %slice-start = ((s8[5242880]{0:T(1024)(128)(4,1)}), s8[4194304]{0:T(1024)(128)(4,1)S(1)}, s32[]{:S(2)}) async-start(s8[5242880]{0:T(1024)(128)(4,1)} %bitcast.35), calls=%async_computation.7 | async-start | bytes 8388608
  177.0 12.1 %slice-start.2 = ((s8[5242880]{0:T(1024)(128)(4,1)}), s8[4194304]{0:T(1024)(128)(4,1)S(1)}, s32[]{:S(2)}) async-start(s8[5242880]{0:T(1024)(128)(4,1)} %bitcast.38), calls=%async_computation.9 | async-start | bytes 8388608
  181.9 5.0 slice-start.1
  181.9 7.2 slice-start.3
  194.2 13.1 %copy-start.3 = (s32[128,2]{0,1:T(2,128)S(1)}, s32[128,2]{0,1:T(2,128)}, u32[]{:S(2)}) copy-start(s32[128,2]{0,1:T(2,128)} %param.21) | copy-start | bytes 3076
  194.2 13.1 %copy-start.4 = (s32[128,2]{0,1:T(2,128)S(1)}, s32[128,2]{0,1:T(2,128)}, u32[]{:S(2)}) copy-start(s32[128,2]{0,1:T(2,128)} %param.22) | copy-start | bytes 3076
  194.2 13.2 %copy-start.5 = (f32[128,2]{0,1:T(2,128)S(1)}, f32[128,2]{0,1:T(2,128)}, u32[]{:S(2)}) copy-start(f32[128,2]{0,1:T(2,128)} %param.23) | copy-start | bytes 3076
  194.2 164.1 %copy-start = (bf16[128,4096]{1,0:T(8,128)(2,1)S(1)}, bf16[128,4096]{1,0:T(8,128)(2,1)}, u32[]{:S(2)}) copy-start(bf16[128,4096]{1,0:T(8,128)(2,1)} %all-gather.4.cloned.1.call-done) | copy-start | bytes 3145732
  194.2 461.1 %all-to-all-start.1 = ((bf16[64,5,4096]{2,1,0:T(8,128)(2,1)}), bf16[64,5,4096]{2,1,0:T(8,128)(2,1)}, u32[]{:S(2)}, u32[]{:S(2)}) async-start(bf16[64,5,4096]{2,1,0:T(8,128)(2,1)} %convert_element_type.49), calls=%async_computation.1 | async-start | bytes 8388608 | tf_op jit(solution)/shard_map/all_to_all | solution.py:83
  206.8 558.1 %reduce-scatter.2.cloned.1.call-start = ((), (), s32[]{:S(2)}) async-start(), calls=%async_computation.6 | async-start | bytes 1310720 | tf_op jit(solution)/shard_map/reduce_scatter | solution.py:91
  674.8 8.8 %copy-start.1 = (bf16[128,640]{1,0:T(8,128)(2,1)S(1)}, bf16[128,640]{1,0:T(8,128)(2,1)}, u32[]{:S(2)}) copy-start(bf16[128,640]{1,0:T(8,128)(2,1)} %param.14) | copy-start | bytes 491524
  683.6 81.3 %copy-start.2 = (bf16[128,1024]{1,0:T(8,128)(2,1)S(1)}, bf16[128,1024]{1,0:T(8,128)(2,1)}, u32[]{:S(2)}) copy-start(bf16[128,1024]{1,0:T(8,128)(2,1)} %param.13) | copy-start | bytes 786436
Sparse Core Ops, SparseCore 0:
  9.2 27.5 all-gather.3
  38.5 319.6 all-gather.7
  360.1 288.4 all-gather.5
  689.1 75.7 reduce-scatter.1
where the time goes:
time: 774 us; the launch traced here: 773 us
  waiting for transfers between devices  652 us (84%)
  local copies, waits for them, and re-layouts  34.9 us (5%)
  matrix products  29.8 us (4%)
  starting transfers between devices  23.6 us (3%)
  other arithmetic  19.4 us (3%)
  between operations  13.4 us (2%)
    all_gather x1, waiting for transfers between devices, body(): lax.all_gather(dense_up, 'expert', axis=0, tiled=True)  287 us
    all_gather x1, waiting for transfers between devices, body(): lax.all_gather(dense_gate, 'expert', axis=0, tiled=True)  151 us
    all_to_all x1, waiting for transfers between devices, body(): lax.all_to_all(pack_slots(whole_rows, flat_slot, groups * capacity, group...  109 us
    reduce_scatter x1, waiting for transfers between devices, body(): lax.psum_scatter(together.astype(jnp.bfloat16), 'tensor', scatter_dimensi...  75.9 us
    all_gather x1, waiting for transfers between devices, body(): whole_rows = lax.all_gather(tokens, 'tensor', axis=1, tiled=True)  27.8 us
  transfers between devices with their start and end apart: 6, of which 5 were waited for; matrix products, arithmetic and copies ran while one was open for 6% of the time, Pallas kernels for 0%

commit v1 on v0

v1 whole, which is shorter than its diff:
```python
import functools

import jax
import jax.numpy as jnp
import numpy as np
from jax import lax
from jax.experimental import pallas as pl
from jax.experimental.pallas import tpu as pltpu
from jax.sharding import PartitionSpec as P

MESH = pl.DeviceIdType.MESH
F32, BF16 = jnp.float32, jnp.bfloat16

X, Z = 4, 8
CAP = 5
CHUNKS = 1


def sizes():
    experts = 2 * X * Z
    return experts, experts * CAP, 4 * CAP, X * Z * 4 * CAP


def tables():
    experts, slots, quad, rows = sizes()
    keys = np.zeros((rows,), np.float32)
    first = np.zeros((rows, rows), np.float32)
    second = np.zeros((rows, rows), np.float32)
    for x in range(X):
        for z in range(Z):
            for g in range(2):
                for e in range(2):
                    for s in range(CAP):
                        q = (g * 2 + e) * CAP + s
                        by_xz = (x * Z + z) * quad + q
                        by_zx = (z * X + x) * quad + q
                        keys[by_xz] = g * slots + (e * X * Z + x * Z + z) * CAP + s
                        first[by_zx, by_xz] = 1.0
                        second[e * slots + (g * X * Z + x * Z + z) * CAP + s, by_zx] = 1.0
    key_sub = np.broadcast_to(keys[:, None], (rows, 128)).astype(np.float32)
    key_lane = np.broadcast_to(keys[None, :], (8, rows)).astype(np.float32)
    perms = np.stack([first, second, second.T, first.T])
    return key_sub, key_lane, perms


def backs(gate, up, upstream):
    s = jax.nn.sigmoid(gate)
    weighted = upstream * s
    return weighted * up * (1.0 + gate * (1.0 - s)), weighted * gate


def nt(a, b):
    return lax.dot_general(a, b, (((1,), (1,)), ((), ())), preferred_element_type=F32)


def dot(a, b):
    return jnp.dot(a, b, preferred_element_type=F32)


def kernel(
    tok, route, wsplit, hid, eg, eu, eh, res, key_sub, key_lane, perms_in,
    out,
    T, RT, H, Wd, Wx, perms, S, B1, B1p, B2, B2p, Xe, Eback, Esib_s, Esib_r, Ex_s, Ex_r, Rb, R2, ZB, ZBp, XB,
    Dback, Dsib_s, Dsib_r, Dx_s, Dx_r, Down, Fin, Fs, Fr,
    send, recv, local,
):
    experts, slots, quad, rows = sizes()
    n_tok, dq = tok.shape
    db = dq // 2
    dc = db // CHUNKS
    rb = wsplit.shape[1]
    e = lax.axis_index("expert")
    t = lax.axis_index("tensor")
    yl, x, z = e // (X * Z), lax.rem(e // Z, X), lax.rem(e, Z)
    yh, c = t // 2, lax.rem(t, 2)

    def dev(yl_, x_, z_, yh_, c_):
        return (yl_ * (X * Z) + x_ * Z + z_, yh_ * 2 + c_)

    def colblk(yl_, yh_, c_):
        return pl.multiple_of((yh_ * 2 + c_) * dq + yl_ * db, db)

    def xr(d):
        return lax.rem(x + d, X)

    def zr(d):
        return lax.rem(z + d + Z, Z)

    partner = dev(1 - yl, x, z, yh, c)
    sibling = dev(yl, x, z, yh, 1 - c)
    others = [(1, 0), (1, 1), (0, 1)]

    def chip(dyl, dyh):
        return (1 - yl if dyl else yl), (1 - yh if dyh else yh)

    pending = []

    def push(src, dst, device):
        i = len(pending)
        copy = pltpu.make_async_remote_copy(
            src_ref=src, dst_ref=dst, send_sem=send.at[i], recv_sem=recv.at[i],
            device_id=device, device_id_type=MESH,
        )
        copy.start()
        pending.append(copy)
        return copy

    locals_ = []

    def load(src, dst):
        copy = pltpu.make_async_copy(src, dst, local.at[len(locals_)])
        copy.start()
        locals_.append(copy)
        return copy

    perm_loads = [load(perms_in, perms)]
    weight_loads = []
    n_tiles = eg.shape[1] // 128
    for j in range(n_tiles):
        weight_loads.append(load(eg.at[:, pl.ds(j * 128, 128)], Wx.at[:, pl.ds(j * 256, 128)]))
        weight_loads.append(load(eu.at[:, pl.ds(j * 128, 128)], Wx.at[:, pl.ds(j * 256 + 128, 128)]))

    barrier = pltpu.get_barrier_semaphore()
    peers = [dev(yl_, x, z, yh_, c_) for dyl, dyh in others for yl_, yh_ in [chip(dyl, dyh)] for c_ in (c, 1 - c)]
    peers += [sibling]
    peers += [dev(yl, xr(d), z, yh, c) for d in range(1, X)]
    peers += [dev(yl, x, zr(d), yh, c) for d in range(1, Z)]
    for peer in peers:
        pl.semaphore_signal(barrier, inc=1, device_id=peer, device_id_type=MESH)
    pl.semaphore_wait(barrier, len(peers))

    my_cols = pl.multiple_of(t * dq, dq)
    own_half = pl.multiple_of(yl * db, db)
    oth_half = pl.multiple_of((1 - yl) * db, db)
    sw_route = push(route, RT.at[yl], partner)
    sw_tok = push(tok.at[:, pl.ds(oth_half, db)], T.at[yl, :, pl.ds(my_cols + oth_half, db)], partner)
    sw_w = push(wsplit.at[1 - yl], Wd.at[yl, x, z], partner)
    sw_h = push(hid.at[1 - yl], H.at[yl], partner)

    RT[yl] = route[...]
    T[yl, :, pl.ds(my_cols, dq)] = tok[...]
    Wd[yl, x, z] = wsplit[yl]
    H[yl] = hid[yl]

    sw_route.wait_recv()
    picks = []
    for g in range(2):
        codes = RT[g]
        hit = (key_sub[...] == codes[0:1, :] + g * slots) | (key_sub[...] == codes[1:2, :] + g * slots)
        picks.append(jnp.where(hit, 1.0, 0.0).astype(BF16))
    sw_tok.wait_recv()
    mine = colblk(yl, yh, c)
    x_copies = []
    for h in range(CHUNKS):
        lanes = pl.ds(pl.multiple_of(mine + h * dc, dc), dc)
        packed = (dot(picks[0], T[0, :, lanes]) + dot(picks[1], T[1, :, lanes])).astype(BF16)
        S[h] = packed.reshape(X, Z * quad, dc)
        for d in (1, X - 1, *range(2, X - 1)) if X > 2 else (1,):
            x_copies.append(push(S.at[h, xr(d)], B1.at[h, x], dev(yl, xr(d), z, yh, c)))
        B1[h, x] = S[h, x]

    t_first = [push(tok.at[:, pl.ds(own_half, db)], T.at[yl, :, pl.ds(my_cols + own_half, db)], partner)]
    t_sib = [push(tok, T.at[yl, :, pl.ds(my_cols, dq)], sibling)]
    for dyl, dyh in others[1:]:
        yl_, yh_ = chip(dyl, dyh)
        t_first.append(push(tok, T.at[yl, :, pl.ds(my_cols, dq)], dev(yl_, x, z, yh_, c)))

    fwd_steps, bwd_steps = Z // 2, (Z - 1) // 2
    a_fwd, a_bwd, a_x, b_x, b_fwd, b_bwd = [], [], [], [], [], []
    z_next, z_prev = dev(yl, x, zr(1), yh, c), dev(yl, x, zr(-1), yh, c)

    def a_spread(zz):
        for d in range(1, X):
            a_x.append(push(Wd.at[0, x, zz], Wd.at[0, x, zz], dev(yl, xr(d), z, yh, c)))

    def ag_start():
        sw_w.wait_recv()
        for d in range(1, X):
            b_x.append(push(Wd.at[1, x, z], Wd.at[1, x, z], dev(yl, xr(d), z, yh, c)))
        a_fwd.append(push(Wd.at[0, x, z], Wd.at[0, x, z], z_next))
        if bwd_steps:
            a_bwd.append(push(Wd.at[0, x, z], Wd.at[0, x, z], z_prev))
        a_spread(z)

    def b_start():
        for copy in b_x:
            copy.wait_recv()
        b_fwd.append(push(Wd.at[1, :, z], Wd.at[1, :, z], z_next))
        if bwd_steps:
            b_bwd.append(push(Wd.at[1, :, z], Wd.at[1, :, z], z_prev))

    def a_step(s):
        def run():
            a_fwd[s - 1].wait_recv()
            zz = zr(-s)
            if s < fwd_steps:
                a_fwd.append(push(Wd.at[0, x, zz], Wd.at[0, x, zz], z_next))
            a_spread(zz)
            if s <= bwd_steps:
                a_bwd[s - 1].wait_recv()
                zz = zr(s)
                if s < bwd_steps:
                    a_bwd.append(push(Wd.at[0, x, zz], Wd.at[0, x, zz], z_prev))
                a_spread(zz)
        return run

    def b_step(s):
        def run():
            b_fwd[s - 1].wait_recv()
            if s < fwd_steps:
                zz = zr(-s)
                b_fwd.append(push(Wd.at[1, :, zz], Wd.at[1, :, zz], z_next))
            if s <= bwd_steps:
                b_bwd[s - 1].wait_recv()
                if s < bwd_steps:
                    zz = zr(s)
                    b_bwd.append(push(Wd.at[1, :, zz], Wd.at[1, :, zz], z_prev))
        return run

    ag_tasks = [ag_start, b_start]
    for s in range(1, fwd_steps + 1):
        ag_tasks += [a_step(s), b_step(s)]

    def service(n=1):
        for _ in range(n):
            if ag_tasks:
                ag_tasks.pop(0)()

    for load_ in perm_loads:
        load_.wait()
    z_order = sorted(range(1, Z), key=lambda d: -min(d, Z - d))
    z_copies = []
    for h in range(CHUNKS):
        for copy in x_copies[h * (X - 1):(h + 1) * (X - 1)]:
            copy.wait_recv()
        B1p[h] = dot(perms[0], B1[h].reshape(rows, dc)).astype(BF16).reshape(Z, X * quad, dc)
        for d in z_order:
            z_copies.append(push(B1p.at[h, zr(d)], B2.at[h, z], dev(yl, x, zr(d), yh, c)))
        B2[h, z] = B1p[h, z]

    service(1)
    for (dyl, dyh), copy in zip(others, t_first):
        copy.wait_recv()
        yl_, yh_ = chip(dyl, dyh)
        cols = pl.ds(pl.multiple_of((yh_ * 2 + c) * dq, dq), dq)
        t_sib.append(push(T.at[yl_, :, cols], T.at[yl_, :, cols], sibling))
    service(1)

    y_copies, y_sib = [], []
    for h in range(CHUNKS):
        for copy in z_copies[h * (Z - 1):(h + 1) * (Z - 1)]:
            copy.wait_recv()
        B2p[h] = dot(perms[1], B2[h].reshape(rows, dc)).astype(BF16).reshape(2, slots, dc)
        here = pl.ds(pl.multiple_of(mine + h * dc, dc), dc)
        for dyl, dyh in (others[2], others[0], others[1]):
            yl_, yh_ = chip(dyl, dyh)
            y_copies.append(((dyl, dyh), push(B2p.at[h, yl_], Xe.at[:, here], dev(yl_, x, z, yh_, c))))
        y_sib.append(push(B2p.at[h, yl], Xe.at[:, here], sibling))
        Xe[:, here] = B2p[h, yl]
    service(2)
    for i, ((dyl, dyh), copy) in enumerate(y_copies):
        h = i // 3
        copy.wait_recv()
        yl_, yh_ = chip(dyl, dyh)
        cols = pl.ds(pl.multiple_of(colblk(yl_, yh_, c) + h * dc, dc), dc)
        y_sib.append(push(Xe.at[:, cols], Xe.at[:, cols], sibling))
        service(1)
    for copy in weight_loads:
        copy.wait()
    for copy in y_sib:
        copy.wait_recv()

    for j in range(n_tiles):
        pre = dot(Xe[...], Wx[:, pl.ds(j * 256, 256)])
        upstream = eh[:, pl.ds(j * 128, 128)].astype(F32)
        gate_back, up_back = backs(pre[:, :128], pre[:, 128:], upstream)
        Eback[:, pl.ds(j * 256, 128)] = gate_back.astype(BF16)
        Eback[:, pl.ds(j * 256 + 128, 128)] = up_back.astype(BF16)
        service(1)

    targets = [(0, 1), (1, 0), (1, 1), (0, 0)]
    e_sib, e_x = {}, {}
    for h in range(CHUNKS):
        for i, (dyl, dyh) in enumerate(targets):
            yl_, yh_ = chip(dyl, dyh)
            r0 = pl.multiple_of(colblk(yl_, yh_, 1 - c) + h * dc, dc)
            Esib_s[h, i] = nt(Eback[...], Wx[pl.ds(r0, dc), :]).astype(BF16)
            e_sib[h, i] = push(Esib_s.at[h, i], Esib_r.at[h, i], sibling)
        for i, (dyl, dyh) in enumerate(targets):
            yl_, yh_ = chip(dyl, dyh)
            r0 = pl.multiple_of(colblk(yl_, yh_, c) + h * dc, dc)
            part = nt(Eback[...], Wx[pl.ds(r0, dc), :])
            e_sib[h, i].wait_recv()
            total = part + Esib_r[h, i].astype(F32)
            if i < 3:
                Ex_s[h, i] = total.astype(BF16)
                e_x[h, i] = push(Ex_s.at[h, i], Ex_r.at[h, i], dev(yl_, x, z, yh_, c))
            else:
                Rb[h] = total

    service(len(ag_tasks))
    sw_h.wait_recv()
    for copy in t_sib:
        copy.wait_recv()
    for copy in a_x:
        copy.wait_recv()
    tokens = T[...].reshape(2 * n_tok, T.shape[2])
    for j in range(2):
        w = Wd[:, :, :, :, pl.ds(j * 256, 256)].reshape(Wd.shape[0] * X * Z * rb, 256)
        pre = dot(tokens, w)
        upstream = H[:, :, pl.ds(j * 128, 128)].reshape(2 * n_tok, 128).astype(F32)
        gate_back, up_back = backs(pre[:, :128], pre[:, 128:], upstream)
        Dback[:, pl.ds(j * 256, 128)] = gate_back.astype(BF16)
        Dback[:, pl.ds(j * 256 + 128, 128)] = up_back.astype(BF16)
    w = Wd[:, :, :, :, pl.ds(512, 128)].reshape(Wd.shape[0] * X * Z * rb, 128)
    pre = dot(tokens, w)
    turned = pltpu.roll(pre, 64, axis=1)
    low = lax.broadcasted_iota(jnp.int32, pre.shape, 1) < 64
    upstream = H[:, :, pl.ds(256, 128)].reshape(2 * n_tok, 128).astype(F32)
    gate_back, up_back = backs(jnp.where(low, pre, turned), jnp.where(low, turned, pre), upstream)
    Dback[:, pl.ds(512, 128)] = jnp.where(low, gate_back, up_back).astype(BF16)

    blocks_per = db // rb

    def dense_rows(yl_, yh_, c_):
        first = ((yh_ * 2 + c_) * 2 + yl_) * blocks_per
        return Wf(first)

    def Wf(first):
        yy, rest = first // (X * Z), lax.rem(first, X * Z)
        xx, zz = rest // Z, lax.rem(rest, Z)
        return Wd[yy, xx, pl.ds(zz, blocks_per)].reshape(db, Wd.shape[4])

    d_sib, d_x = {}, {}
    for i, (dyl, dyh) in enumerate(targets):
        yl_, yh_ = chip(dyl, dyh)
        Dsib_s[i] = nt(Dback[...], dense_rows(yl_, yh_, 1 - c)).astype(BF16)
        d_sib[i] = push(Dsib_s.at[i], Dsib_r.at[i], sibling)
    for i, (dyl, dyh) in enumerate(targets):
        yl_, yh_ = chip(dyl, dyh)
        part = nt(Dback[...], dense_rows(yl_, yh_, c))
        d_sib[i].wait_recv()
        total = part + Dsib_r[i].astype(F32)
        if i < 3:
            Dx_s[i] = total.astype(BF16)
            d_x[i] = push(Dx_s.at[i], Dx_r.at[i], dev(yl_, x, z, yh_, c))
        else:
            Down[...] = total

    zb, xb = [], []
    for h in range(CHUNKS):
        for i in range(3):
            e_x[h, i].wait_recv()
        R2[h, yl] = (Rb[h] + Ex_r[h, 0].astype(F32)).astype(BF16)
        R2[h, 1 - yl] = (Ex_r[h, 1].astype(F32) + Ex_r[h, 2].astype(F32)).astype(BF16)
        B1p2 = dot(perms[2], R2[h].reshape(rows, dc)).astype(BF16).reshape(Z, X * quad, dc)
        B2[h] = B1p2
        for d in z_order:
            zb.append(push(B2.at[h, zr(d)], ZB.at[h, z], dev(yl, x, zr(d), yh, c)))
        ZB[h, z] = B2[h, z]
    for h in range(CHUNKS):
        for copy in zb[h * (Z - 1):(h + 1) * (Z - 1)]:
            copy.wait_recv()
        ZBp[h] = dot(perms[3], ZB[h].reshape(rows, dc)).astype(BF16).reshape(X, Z * quad, dc)
        for d in (1, X - 1, *range(2, X - 1)) if X > 2 else (1,):
            xb.append(push(ZBp.at[h, xr(d)], XB.at[h, x], dev(yl, xr(d), z, yh, c)))
        XB[h, x] = ZBp[h, x]

    for i in range(3):
        d_x[i].wait_recv()
    Fin[...] = Down[...] + Dx_r[0].astype(F32) + Dx_r[1].astype(F32) + Dx_r[2].astype(F32)
    picks = []
    for g in range(2):
        codes = jnp.concatenate([RT[g], jnp.zeros((120, 128), F32)], axis=0).T
        picks.append(
            [
                (
                    jnp.where(key_lane[0:1, :] == codes[:, k:k + 1] + g * slots, 1.0, 0.0).astype(BF16),
                    codes[:, 2 + k:3 + k],
                )
                for k in range(2)
            ]
        )
    for h in range(CHUNKS):
        for copy in xb[h * (X - 1):(h + 1) * (X - 1)]:
            copy.wait_recv()
        returned = XB[h].reshape(rows, dc)
        for g in range(2):
            total = Fin[pl.ds(g * n_tok, n_tok), pl.ds(h * dc, dc)]
            for hot, weight in picks[g]:
                total = total + weight * dot(hot, returned)
            Fin[pl.ds(g * n_tok, n_tok), pl.ds(h * dc, dc)] = total
    own_rows = pl.ds(pl.multiple_of(yl * n_tok, n_tok), n_tok)
    oth_rows = pl.ds(pl.multiple_of((1 - yl) * n_tok, n_tok), n_tok)
    Fs[...] = Fin[oth_rows, :].astype(BF16)
    last = push(Fs, Fr, partner)
    out[:, pl.ds(own_half, db)] = (res[:, pl.ds(own_half, db)].astype(F32) + Fin[own_rows, :]).astype(BF16)
    last.wait_recv()
    out[:, pl.ds(oth_half, db)] = (res[:, pl.ds(oth_half, db)].astype(F32) + Fr[...].astype(F32)).astype(BF16)
    for copy in pending:
        copy.wait_send()


N_SEMS = 140


def run_kernel(tok, route, wsplit, hid, eg, eu, eh, res):
    experts, slots, quad, rows = sizes()
    n_tok, dq = tok.shape
    d = dq * 4
    db = dq // 2
    dc = db // CHUNKS
    rb = wsplit.shape[1]
    key_sub, key_lane, perms = tables()
    vm = pl.BlockSpec(memory_space=pltpu.VMEM)
    hbm = pl.BlockSpec(memory_space=pl.ANY)
    V = pltpu.VMEM
    C = CHUNKS
    wide = eg.shape[1] * 2
    return pl.pallas_call(
        kernel,
        out_shape=jax.ShapeDtypeStruct((n_tok, dq), BF16),
        in_specs=[vm, vm, vm, vm, hbm, hbm, vm, vm, vm, vm, hbm],
        out_specs=vm,
        scratch_shapes=[
            V((2, n_tok, d), BF16),
            V((2, 8, 128), F32),
            V((2, n_tok, 384), BF16),
            V((2, X, Z, rb, 640), BF16),
            V((d, wide), BF16),
            V((4, rows, rows), BF16),
            V((C, X, Z * quad, dc), BF16),
            V((C, X, Z * quad, dc), BF16),
            V((C, Z, X * quad, dc), BF16),
            V((C, Z, X * quad, dc), BF16),
            V((C, 2, slots, dc), BF16),
            V((slots, d), BF16),
            V((slots, wide), BF16),
            V((C, 4, slots, dc), BF16),
            V((C, 4, slots, dc), BF16),
            V((C, 3, slots, dc), BF16),
            V((C, 3, slots, dc), BF16),
            V((C, slots, dc), F32),
            V((C, 2, slots, dc), BF16),
            V((C, Z, X * quad, dc), BF16),
            V((C, X, Z * quad, dc), BF16),
            V((C, X, Z * quad, dc), BF16),
            V((2 * n_tok, 640), BF16),
            V((4, 2 * n_tok, db), BF16),
            V((4, 2 * n_tok, db), BF16),
            V((3, 2 * n_tok, db), BF16),
            V((3, 2 * n_tok, db), BF16),
            V((2 * n_tok, db), F32),
            V((2 * n_tok, db), F32),
            V((n_tok, db), BF16),
            V((n_tok, db), BF16),
            pltpu.SemaphoreType.DMA((N_SEMS,)),
            pltpu.SemaphoreType.DMA((N_SEMS,)),
            pltpu.SemaphoreType.DMA((16,)),
        ],
        compiler_params=pltpu.CompilerParams(
            collective_id=0, has_side_effects=True, vmem_limit_bytes=60 * 1024 * 1024
        ),
    )(
        tok, route, wsplit, hid, eg, eu, eh, res,
        jnp.asarray(key_sub), jnp.asarray(key_lane), jnp.asarray(perms, BF16),
    )


def body(
    tokens,
    residual_grad,
    dense_hidden,
    dense_gate,
    dense_up,
    expert_gate,
    expert_up,
    expert_hidden,
    expert_ids,
    slot_index,
    kept_mask,
    gate_weights,
):
    take = (kept_mask == 1) & (slot_index < CAP)
    code = jnp.where(take, expert_ids * CAP + slot_index, -100000).astype(F32)
    weight = jnp.where(take, gate_weights, 0.0)
    route = jnp.concatenate([code, weight, jnp.zeros((code.shape[0], 4), F32)], axis=1).T
    halves, hidden = [], []
    for h in range(2):
        o = h * 320
        halves.append(
            jnp.concatenate(
                [
                    dense_gate[:, o:o + 128], dense_up[:, o:o + 128],
                    dense_gate[:, o + 128:o + 256], dense_up[:, o + 128:o + 256],
                    dense_gate[:, o + 256:o + 320], dense_up[:, o + 256:o + 320],
                ],
                axis=1,
            )
        )
        hidden.append(
            jnp.concatenate([dense_hidden[:, o:o + 320], dense_hidden[:, o + 256:o + 320]], axis=1)
        )
    return run_kernel(
        tokens, route, jnp.stack(halves), jnp.stack(hidden),
        expert_gate[0], expert_up[0], expert_hidden[0], residual_grad,
    )


def solution(mesh):
    both = P("expert", "tensor")
    rows = P("expert", None)
    last = P("expert", None, "tensor")
    placed = (both, both, both, both, both, last, last, last, rows, rows, rows, rows)
    return jax.shard_map(body, mesh=mesh, in_specs=placed, out_specs=both, check_vma=False)
```

time: 774 us -> 141 us (0.18)
  waiting for transfers between devices: 652 us -> 0 us
  Pallas kernels: 0 us -> 129 us
  matrix products: 29.8 us -> 0 us
  local copies, waits for them, and re-layouts: 34.9 us -> 5.66 us
  starting transfers between devices: 23.6 us -> 0 us
  other arithmetic: 19.4 us -> 3.56 us
  between operations: 13.4 us -> 0.04 us
    all_gather x3 -> x0, waiting for transfers between devices: 465 us -> none  [the longest x1 287 us: body(): lax.all_gather(dense_up, 'expert', axis=0, tiled=True)]
    pallas_call x0 -> x1, Pallas kernels: none -> 129 us  [run_kernel(): pl.pallas_call(kernel, out_shape=jax.ShapeDtypeStruct((n_tok, dq), BF16),...]
    all_to_all x2 -> x0, waiting for transfers between devices: 109 us -> none  [the longest x1 109 us: body(): lax.all_to_all(pack_slots(whole_rows, flat_slot, groups * capacity, group...]
    reduce_scatter x1 -> x0, waiting for transfers between devices: 75.9 us -> none  [body(): lax.psum_scatter(together.astype(jnp.bfloat16), 'tensor', scatter_dimensi...]
    dot_general x7 -> x0, matrix products: 29.8 us -> none  [the longest x2 8.98 us: project_back(): jnp.einsum('tf,df->td', gate_back, gate_matrix, preferred_element_type=jn...]
    all_to_all x2 -> x0, starting transfers between devices: 23 us -> none  [the longest x1 12.6 us: body(): lax.all_to_all(expert_part.reshape(groups, capacity, expert_part.shape[1]...]
    gather x2 -> x0, local copies, waits for them, and re-layouts: 14.1 us -> none  [combine(): picked = buffer[jnp.minimum(flat_slot, buffer.shape[0] - 1)]]
    reshape x5 -> x0, local copies, waits for them, and re-layouts: 14 us -> none  [the longest x1 5.34 us: combine(): buffer = returned.reshape(-1, returned.shape[-1])]
  transfers between devices with their start and end apart: 6 -> 0, of which waited for: 5 -> 0; matrix products, arithmetic and copies ran while one was open for 6% -> 0% of each run, Pallas kernels for 0% -> 0%
where the time goes in v1:
time: 141 us; the launch traced here: 138 us
  Pallas kernels  129 us (91%)
  local copies, waits for them, and re-layouts  5.66 us (4%)
  other arithmetic  3.56 us (3%)
    pallas_call x1, Pallas kernels, run_kernel(): pl.pallas_call(kernel, out_shape=jax.ShapeDtypeStruct((n_tok, dq), BF16),...  129 us

profile of v1, /device:TPU:1, one launch (start us, length us, event | category | flops | bytes accessed | tf_op | source)
XLA Modules:
  0.0 138.2 jit_solution(15615880938389408576)
XLA Ops:
  0.0 0.9 fusion.4
  0.9 0.9 fusion.2
  1.8 0.1 concatenate.16
  1.9 0.1 concatenate.17
  2.0 0.7 pad_maximum_fusion.1.wsplit
  2.7 1.1 fusion
  3.8 0.9 fusion.1
  4.6 0.1 maximum_bitcast_fusion
  4.7 0.7 pad_maximum_fusion.hid
  5.4 0.7 broadcast_select_fusion
  6.1 0.1 pad.10.clone
  6.2 0.7 select_convert_fusion
  6.9 0.7 maximum_bitcast_fusion.2.route
  7.6 129.0 %shard_map.145 = bf16[128,1024]{1,0:T(8,128)(2,1)} custom-call(bf16[128,1024]{1,0:T(8,128)(2,1)} %tok.1, f32[8,128]{1,0:T(8,128)} %maximum_bitcast_fusion.2.route, bf16[2,64,640]{2,1,0:T(8,128)(2,1)} %pad_maximum_fusion.1.wsplit, bf16[2,128,384]{2,1,0:T(8,128)(2,1)} %pad_maximum_fusion.hid, bf16[4096,640]{1,0:T(8,128)(2,1)} %bitcast.11, ...), custom_call_target="tpu_custom_call" | custom-call | tf_op jit(solution)/shard_map/pallas_call | solution.py:420
  136.5 1.7 %copy.17 = bf16[128,1024]{1,0:T(8,128)(2,1)} copy(bf16[128,1024]{1,0:T(8,128)(2,1)} %shard_map.145) | data formatting | bytes 524288
  (1 shorter events, 0.0 us)

commit v2 on v0

v2 whole, which is shorter than its diff:
```python
import functools

import jax
import jax.numpy as jnp
import numpy as np
from jax import lax
from jax.experimental import pallas as pl
from jax.experimental.pallas import tpu as pltpu
from jax.sharding import PartitionSpec as P

MESH = pl.DeviceIdType.MESH
F32, BF16 = jnp.float32, jnp.bfloat16

X, Z = 4, 8
CAP = 5
CHUNKS = 2


def sizes():
    experts = 2 * X * Z
    return experts, experts * CAP, 2 * CAP, 2 * experts * CAP


def tables():
    experts, slots, ten, rows = sizes()
    keys = np.zeros((rows,), np.float32)
    first = np.zeros((rows, rows), np.float32)
    second = np.zeros((rows, rows), np.float32)
    for x in range(X):
        for z in range(Z):
            for e in range(2):
                for s in range(CAP):
                    by_xz = (x * Z + z) * ten + e * CAP + s
                    keys[by_xz] = (e * X * Z + x * Z + z) * CAP + s
                    for half in range(2):
                        by_zx = (z * 2 + half) * X * ten + x * ten + e * CAP + s
                        first[by_zx, half * slots + by_xz] = 1.0
                        second[half * slots + e * (slots // 2) + (x * Z + z) * CAP + s, by_zx] = 1.0
    columns = np.zeros((rows, 128), np.float32)
    columns[:, 0] = keys
    for k, order in enumerate((first, second, second.T, first.T)):
        columns[:, 1 + k] = np.argmax(order, axis=1)
    key_lane = np.broadcast_to(keys[None, :slots], (8, slots)).astype(np.float32)
    return columns, key_lane


def backs(gate, up, upstream):
    s = jax.nn.sigmoid(gate)
    weighted = upstream * s
    return weighted * up * (1.0 + gate * (1.0 - s)), weighted * gate


def nt(a, b):
    return lax.dot_general(a, b, (((1,), (1,)), ((), ())), preferred_element_type=F32)


def dot(a, b):
    return jnp.dot(a, b, preferred_element_type=F32)


def stack(v):
    w = v.shape[1] // 2
    return jnp.concatenate([v[:, :w], v[:, w:]], axis=0)


def spread(v):
    n = v.shape[0] // 2
    return jnp.concatenate([v[:n], v[n:]], axis=1)


def kernel(
    tok, ids, slot, kept, gate_w, dg, du, dh, eg, eu, eh, res, table, key_lane,
    out,
    T, Ws, Hs, H, Wd, Wx, perms, S, B1, B1p, B2, B2p, Xe, Epre, Eback, Esib_s, Esib_r, Ex_s, Ex_r, Etot, R2,
    Z2, ZB, ZBp, XB, Dback, Dsib_s, Dsib_r, Dx_s, Dx_r, Dtot,
    send, recv, local,
):
    experts, slots, ten, rows = sizes()
    half = slots // 2
    n_tok, dq = tok.shape
    dc = dq // CHUNKS
    w = dc // 2
    rb = dg.shape[0]
    e = lax.axis_index("expert")
    t = lax.axis_index("tensor")
    yl, x, z = e // (X * Z), lax.rem(e // Z, X), lax.rem(e, Z)
    yh, c = t // 2, lax.rem(t, 2)

    def dev(yl_, x_, z_, yh_, c_):
        return (yl_ * (X * Z) + x_ * Z + z_, yh_ * 2 + c_)

    def lanes(t_, width):
        return pl.ds(pl.multiple_of(t_ * width, width), width)

    def xr(d):
        return lax.rem(x + d, X)

    def zr(d):
        return lax.rem(z + d + Z, Z)

    partner = dev(1 - yl, x, z, yh, c)
    sibling = dev(yl, x, z, yh, 1 - c)
    others = [(0, 1), (1, 0), (1, 1)]

    def chip(dyl, dyh):
        return (1 - yl if dyl else yl), (1 - yh if dyh else yh)

    pending = []

    def push(src, dst, device):
        i = len(pending)
        copy = pltpu.make_async_remote_copy(
            src_ref=src, dst_ref=dst, send_sem=send.at[i], recv_sem=recv.at[i],
            device_id=device, device_id_type=MESH,
        )
        copy.start()
        pending.append(copy)
        return copy

    locals_ = []

    def load(src, dst):
        copy = pltpu.make_async_copy(src, dst, local.at[len(locals_)])
        copy.start()
        locals_.append(copy)
        return copy

    barrier = pltpu.get_barrier_semaphore()
    peers = [dev(yl, xr(d), z, yh, c) for d in range(1, X)]
    peers += [dev(yl, x, zr(d), yh, c) for d in range(1, Z)]
    for dyl, dyh in others:
        yl_, yh_ = chip(dyl, dyh)
        peers += [dev(yl_, x, z, yh_, c)]
    peers += [sibling]
    for peer in peers:
        pl.semaphore_signal(barrier, inc=1, device_id=peer, device_id_type=MESH)

    weight_loads = []
    n_tiles = eg.shape[3] // 128
    for j in range(n_tiles):
        weight_loads.append(load(eg.at[:, :, :, pl.ds(j * 128, 128)], Wx.at[:, :, :, pl.ds(j * 256, 128)]))
        weight_loads.append(load(eu.at[:, :, :, pl.ds(j * 128, 128)], Wx.at[:, :, :, pl.ds(j * 256 + 128, 128)]))

    take = (kept[...] == 1) & (slot[...] < CAP)
    code = jnp.where(take, ids[...] * CAP + slot[...], -100000).astype(F32)
    weight = jnp.where(take, gate_w[...], 0.0)
    keys = table[pl.ds(0, slots), 0:1]
    pick = jnp.where((keys == code[0:1, :]) | (keys == code[1:2, :]), 1.0, 0.0).astype(BF16)
    for h in range(CHUNKS):
        S[h] = dot(pick, tok[:, pl.ds(h * dc, dc)]).astype(BF16).reshape(X, Z * ten, dc)
    pl.semaphore_wait(barrier, len(peers))
    x_order = sorted(range(1, X), key=lambda d: -min(d, X - d))
    z_order = sorted(range(1, Z), key=lambda d: -min(d, Z - d))
    x_copies = [[push(S.at[h, xr(d)], B1.at[h, x], dev(yl, xr(d), z, yh, c)) for d in x_order] for h in range(CHUNKS)]
    for h in range(CHUNKS):
        B1[h, x] = S[h, x]

    def low(rows_):
        return lax.broadcasted_iota(jnp.int32, (rows_, 128), 1) < 64

    g_last, u_last = dg[:, pl.ds(512, 128)].astype(F32), du[:, pl.ds(512, 128)].astype(F32)
    h_last = dh[:, pl.ds(512, 128)].astype(F32)
    h_turned = pltpu.roll(h_last, 64, axis=1)
    for h in range(2):
        for j in range(2):
            Ws[h, :, pl.ds(j * 256, 128)] = dg[:, pl.ds((h * 2 + j) * 128, 128)]
            Ws[h, :, pl.ds(j * 256 + 128, 128)] = du[:, pl.ds((h * 2 + j) * 128, 128)]
        Hs[h, :, pl.ds(0, 256)] = dh[:, pl.ds(h * 256, 256)]
    Ws[0, :, pl.ds(512, 128)] = jnp.where(low(rb), g_last, pltpu.roll(u_last, 64, axis=1)).astype(BF16)
    Ws[1, :, pl.ds(512, 128)] = jnp.where(low(rb), pltpu.roll(g_last, 64, axis=1), u_last).astype(BF16)
    Hs[0, :, pl.ds(256, 128)] = jnp.where(low(n_tok), h_last, h_turned).astype(BF16)
    Hs[1, :, pl.ds(256, 128)] = jnp.where(low(n_tok), h_turned, h_last).astype(BF16)
    sw_w = push(Ws.at[1 - yl], Wd.at[yl, x, z], partner)
    sw_h = push(Hs.at[1 - yl], H.at[yl], partner)
    Wd[yl, x, z] = Ws[yl]
    H[yl] = Hs[yl]

    T[yl, :, lanes(t, dq)] = tok[...]
    t_sib = [push(tok, T.at[yl, :, lanes(t, dq)], sibling)]
    t_first = []
    for dyl, dyh in others:
        yl_, yh_ = chip(dyl, dyh)
        t_first.append(push(tok, T.at[yl, :, lanes(t, dq)], dev(yl_, x, z, yh_, c)))

    fwd_steps, bwd_steps = Z // 2, (Z - 1) // 2
    a_fwd, a_bwd, a_x, b_x, b_fwd, b_bwd = [], [], [], [], [], []
    z_next, z_prev = dev(yl, x, zr(1), yh, c), dev(yl, x, zr(-1), yh, c)

    def a_spread(zz):
        for d in x_order:
            a_x.append(push(Wd.at[0, x, zz], Wd.at[0, x, zz], dev(yl, xr(d), z, yh, c)))

    def ag_start():
        sw_w.wait_recv()
        for d in x_order:
            b_x.append(push(Wd.at[1, x, z], Wd.at[1, x, z], dev(yl, xr(d), z, yh, c)))
        a_fwd.append(push(Wd.at[0, x, z], Wd.at[0, x, z], z_next))
        if bwd_steps:
            a_bwd.append(push(Wd.at[0, x, z], Wd.at[0, x, z], z_prev))
        a_spread(z)

    def b_start():
        for copy in b_x:
            copy.wait_recv()
        b_fwd.append(push(Wd.at[1, :, z], Wd.at[1, :, z], z_next))
        if bwd_steps:
            b_bwd.append(push(Wd.at[1, :, z], Wd.at[1, :, z], z_prev))

    def a_step(s):
        def run():
            a_fwd[s - 1].wait_recv()
            zz = zr(-s)
            if s < fwd_steps:
                a_fwd.append(push(Wd.at[0, x, zz], Wd.at[0, x, zz], z_next))
            a_spread(zz)
            if s <= bwd_steps:
                a_bwd[s - 1].wait_recv()
                zz = zr(s)
                if s < bwd_steps:
                    a_bwd.append(push(Wd.at[0, x, zz], Wd.at[0, x, zz], z_prev))
                a_spread(zz)
        return run

    def b_step(s):
        def run():
            b_fwd[s - 1].wait_recv()
            if s < fwd_steps:
                zz = zr(-s)
                b_fwd.append(push(Wd.at[1, :, zz], Wd.at[1, :, zz], z_next))
            if s <= bwd_steps:
                b_bwd[s - 1].wait_recv()
                if s < bwd_steps:
                    zz = zr(s)
                    b_bwd.append(push(Wd.at[1, :, zz], Wd.at[1, :, zz], z_prev))
        return run

    ag_tasks = [ag_start, b_start]
    for s in range(1, fwd_steps + 1):
        ag_tasks += [a_step(s), b_step(s)]

    def service(place):
        for _ in range(SERVICE.get(place, 0)):
            if ag_tasks:
                ag_tasks.pop(0)()

    def build_order(k):
        across = lax.broadcasted_iota(jnp.int32, (rows, rows), 1).astype(F32)
        perms[k] = jnp.where(across == table[:, 1 + k:2 + k], 1.0, 0.0).astype(BF16)

    build_order(0)
    build_order(1)
    z_copies = []
    for h in range(CHUNKS):
        for copy in x_copies[h]:
            copy.wait_recv()
        B1p[h] = dot(perms[0], stack(B1[h].reshape(slots, dc))).astype(BF16).reshape(Z, 2 * X * ten, w)
        z_copies.append([push(B1p.at[h, zr(d)], B2.at[h, z], dev(yl, x, zr(d), yh, c)) for d in z_order])
        B2[h, z] = B1p[h, z]
        service(f"x{h}")

    for (dyl, dyh), copy in zip(others, t_first):
        copy.wait_recv()
        yl_, yh_ = chip(dyl, dyh)
        held = T.at[yl_, :, lanes(yh_ * 2 + c, dq)]
        t_sib.append(push(held, held, sibling))
    build_order(2)
    build_order(3)
    service("t")

    y_copies, y_sib = [], []
    for h in range(CHUNKS):
        for copy in z_copies[h]:
            copy.wait_recv()
        B2p[h] = spread(dot(perms[1], B2[h].reshape(rows, w))).astype(BF16).reshape(2, half, dc)
        here = Xe.at[h, yl, :, lanes(t, dc)]
        sends = []
        for dyl, dyh in others:
            yl_, yh_ = chip(dyl, dyh)
            sends.append(push(B2p.at[h, yl_], here, dev(yl_, x, z, yh_, c)))
        y_copies.append(sends)
        y_sib.append([push(B2p.at[h, yl], here, sibling)])
        Xe[h, yl, :, lanes(t, dc)] = B2p[h, yl]
        service(f"z{h}")

    for h in range(CHUNKS):
        for i in (1, 2, 0):
            y_copies[h][i].wait_recv()
            yl_, yh_ = chip(*others[i])
            held = Xe.at[h, yl_, :, lanes(yh_ * 2 + c, dc)]
            y_sib[h].append(push(held, held, sibling))
        service(f"y{h}")
        if h == 0:
            for copy in weight_loads:
                copy.wait()
        for copy in y_sib[h]:
            copy.wait_recv()
        for j in range(n_tiles):
            cols = pl.ds(j * 256, 256)
            pre = dot(Xe[h].reshape(slots, 4 * dc), Wx[:, h, :, cols].reshape(4 * dc, 256))
            if h > 0:
                pre = pre + Epre[:, cols]
            if h < CHUNKS - 1:
                Epre[:, cols] = pre
                continue
            upstream = eh[:, pl.ds(j * 128, 128)].astype(F32)
            gate_back, up_back = backs(pre[:, :128], pre[:, 128:], upstream)
            Eback[:, pl.ds(j * 256, 128)] = gate_back.astype(BF16)
            Eback[:, pl.ds(j * 256 + 128, 128)] = up_back.astype(BF16)
        service(f"f{h}")

    e_sib, e_x = {}, {}
    for h in range(CHUNKS):
        for dyh in (1, 0):
            yh_ = chip(0, dyh)[1]
            Esib_s[h, dyh] = nt(Eback[...], Wx[yh_ * 2 + 1 - c, h]).astype(BF16)
            e_sib[h, dyh] = push(Esib_s.at[h, dyh], Esib_r.at[h, dyh], sibling)
        for dyh in (1, 0):
            yh_ = chip(0, dyh)[1]
            part = nt(Eback[...], Wx[yh_ * 2 + c, h])
            e_sib[h, dyh].wait_recv()
            total = (part + Esib_r[h, dyh].astype(F32)).reshape(2, half, dc)
            Ex_s[h, dyh] = total.astype(BF16)
            for dyl in (0, 1):
                if dyl or dyh:
                    yl_ = chip(dyl, dyh)[0]
                    e_x[h, dyl, dyh] = push(Ex_s.at[h, dyh, yl_], Ex_r.at[h, dyl, dyh], dev(yl_, x, z, yh_, c))
            if not dyh:
                Etot[h] = total
        service(f"b{h}")

    def dense_forward():
        sw_h.wait_recv()
        for copy in t_sib:
            copy.wait_recv()
        while ag_tasks:
            ag_tasks.pop(0)()
        for copy in a_x:
            copy.wait_recv()
        tokens = T[...].reshape(2 * n_tok, T.shape[2])
        for j in range(2):
            pre = dot(tokens, Wd[:, :, :, :, pl.ds(j * 256, 256)].reshape(experts * rb, 256))
            upstream = H[:, :, pl.ds(j * 128, 128)].reshape(2 * n_tok, 128).astype(F32)
            gate_back, up_back = backs(pre[:, :128], pre[:, 128:], upstream)
            Dback[:, pl.ds(j * 256, 128)] = gate_back.astype(BF16)
            Dback[:, pl.ds(j * 256 + 128, 128)] = up_back.astype(BF16)
        pre = dot(tokens, Wd[:, :, :, :, pl.ds(512, 128)].reshape(experts * rb, 128))
        turned = pltpu.roll(pre, 64, axis=1)
        low_ = low(2 * n_tok)
        upstream = H[:, :, pl.ds(256, 128)].reshape(2 * n_tok, 128).astype(F32)
        gate_back, up_back = backs(jnp.where(low_, pre, turned), jnp.where(low_, turned, pre), upstream)
        Dback[:, pl.ds(512, 128)] = jnp.where(low_, gate_back, up_back).astype(BF16)

    def dense_share(t_):
        block = Wd[t_ // 2, pl.ds(lax.rem(t_, 2) * (X // 2), X // 2)]
        return nt(Dback[...], block.reshape(dq, 640))

    d_sib, d_x = {}, {}

    def dense_back():
        for dyh in (1, 0):
            yh_ = chip(0, dyh)[1]
            Dsib_s[dyh] = dense_share(yh_ * 2 + 1 - c).astype(BF16).reshape(2, n_tok, dq)
            d_sib[dyh] = push(Dsib_s.at[dyh], Dsib_r.at[dyh], sibling)
        for dyh in (1, 0):
            yh_ = chip(0, dyh)[1]
            part = dense_share(yh_ * 2 + c)
            d_sib[dyh].wait_recv()
            total = part.reshape(2, n_tok, dq) + Dsib_r[dyh].astype(F32)
            Dx_s[dyh] = total.astype(BF16)
            for dyl in (0, 1):
                if dyl or dyh:
                    yl_ = chip(dyl, dyh)[0]
                    d_x[dyl, dyh] = push(Dx_s.at[dyh, yl_], Dx_r.at[dyl, dyh], dev(yl_, x, z, yh_, c))
            if not dyh:
                Dtot[...] = total

    if DENSE == 0:
        dense_forward()
        dense_back()

    z_back = []
    for h in range(CHUNKS):
        for dyl, dyh in others:
            e_x[h, dyl, dyh].wait_recv()
        R2[h, yl] = (Etot[h, yl] + Ex_r[h, 0, 1].astype(F32)).astype(BF16)
        R2[h, 1 - yl] = (Ex_r[h, 1, 0].astype(F32) + Ex_r[h, 1, 1].astype(F32)).astype(BF16)
        Z2[h] = dot(perms[2], stack(R2[h].reshape(slots, dc))).astype(BF16).reshape(Z, 2 * X * ten, w)
        z_back.append([push(Z2.at[h, zr(d)], ZB.at[h, z], dev(yl, x, zr(d), yh, c)) for d in z_order])
        ZB[h, z] = Z2[h, z]
        if DENSE == 1 and h == 0:
            dense_forward()
    if DENSE == 1:
        dense_back()
    if DENSE == 2:
        dense_forward()
        dense_back()
    x_back = []
    for h in range(CHUNKS):
        for copy in z_back[h]:
            copy.wait_recv()
        ZBp[h] = spread(dot(perms[3], ZB[h].reshape(rows, w))).astype(BF16).reshape(X, Z * ten, dc)
        x_back.append([push(ZBp.at[h, xr(d)], XB.at[h, x], dev(yl, xr(d), z, yh, c)) for d in x_order])
        XB[h, x] = ZBp[h, x]

    for dyl, dyh in others:
        d_x[dyl, dyh].wait_recv()
    out_sum = (
        res[...].astype(F32) + Dtot[yl] + Dx_r[0, 1].astype(F32) + Dx_r[1, 0].astype(F32) + Dx_r[1, 1].astype(F32)
    )
    Dtot[0] = out_sum
    down = jnp.concatenate([code, weight, jnp.zeros((124, 128), F32)], axis=0).T
    hots = [jnp.where(key_lane[0:1, :] == down[:, k:k + 1], 1.0, 0.0).astype(BF16) for k in range(2)]
    for h in range(CHUNKS):
        for copy in x_back[h]:
            copy.wait_recv()
        returned = XB[h].reshape(slots, dc)
        total = Dtot[0, :, pl.ds(h * dc, dc)]
        for k in range(2):
            total = total + down[:, 2 + k:3 + k] * dot(hots[k], returned)
        out[:, pl.ds(h * dc, dc)] = total.astype(BF16)
    for copy in pending:
        copy.wait_send()


SERVICE = {"x1": 1, "z1": 1, "y0": 1, "f0": 1, "y1": 1, "f1": 2, "b0": 2, "b1": 1}
DENSE = 1
N_SEMS = 256


def run_kernel(tok, ids, slot, kept, gate_w, dg, du, dh, eg, eu, eh, res):
    experts, slots, ten, rows = sizes()
    half = slots // 2
    n_tok, dq = tok.shape
    d = dq * 4
    dc = dq // CHUNKS
    w = dc // 2
    rb = dg.shape[0]
    table, key_lane = tables()
    vm = pl.BlockSpec(memory_space=pltpu.VMEM)
    hbm = pl.BlockSpec(memory_space=pl.ANY)
    V = pltpu.VMEM
    C = CHUNKS
    wide = eg.shape[1] * 2
    eg, eu = (m.reshape(4, C, dc, m.shape[1]) for m in (eg, eu))
    return pl.pallas_call(
        kernel,
        out_shape=jax.ShapeDtypeStruct((n_tok, dq), BF16),
        in_specs=[vm] * 8 + [hbm, hbm] + [vm] * 4,
        out_specs=vm,
        scratch_shapes=[
            V((2, n_tok, d), BF16),
            V((2, rb, 640), BF16),
            V((2, n_tok, 384), BF16),
            V((2, n_tok, 384), BF16),
            V((2, X, Z, rb, 640), BF16),
            V((4, C, dc, wide), BF16),
            V((4, rows, rows), BF16),
            V((C, X, Z * ten, dc), BF16),
            V((C, X, Z * ten, dc), BF16),
            V((C, Z, 2 * X * ten, w), BF16),
            V((C, Z, 2 * X * ten, w), BF16),
            V((C, 2, half, dc), BF16),
            V((C, 2, half, 4 * dc), BF16),
            V((slots, wide), F32),
            V((slots, wide), BF16),
            V((C, 2, slots, dc), BF16),
            V((C, 2, slots, dc), BF16),
            V((C, 2, 2, half, dc), BF16),
            V((C, 2, 2, half, dc), BF16),
            V((C, 2, half, dc), F32),
            V((C, 2, half, dc), BF16),
            V((C, Z, 2 * X * ten, w), BF16),
            V((C, Z, 2 * X * ten, w), BF16),
            V((C, X, Z * ten, dc), BF16),
            V((C, X, Z * ten, dc), BF16),
            V((2 * n_tok, 640), BF16),
            V((2, 2, n_tok, dq), BF16),
            V((2, 2, n_tok, dq), BF16),
            V((2, 2, n_tok, dq), BF16),
            V((2, 2, n_tok, dq), BF16),
            V((2, n_tok, dq), F32),
            pltpu.SemaphoreType.DMA((N_SEMS,)),
            pltpu.SemaphoreType.DMA((N_SEMS,)),
            pltpu.SemaphoreType.DMA((16,)),
        ],
        compiler_params=pltpu.CompilerParams(
            collective_id=0, has_side_effects=True, vmem_limit_bytes=60 * 1024 * 1024
        ),
    )(
        tok, ids, slot, kept, gate_w, dg, du, dh, eg, eu, eh, res,
        jnp.asarray(table), jnp.asarray(key_lane),
    )


def body(
    tokens,
    residual_grad,
    dense_hidden,
    dense_gate,
    dense_up,
    expert_gate,
    expert_up,
    expert_hidden,
    expert_ids,
    slot_index,
    kept_mask,
    gate_weights,
):
    return run_kernel(
        tokens, expert_ids.T, slot_index.T, kept_mask.T, gate_weights.T, dense_gate, dense_up, dense_hidden,
        expert_gate[0], expert_up[0], expert_hidden[0], residual_grad,
    )


def solution(mesh):
    both = P("expert", "tensor")
    rows = P("expert", None)
    last = P("expert", None, "tensor")
    placed = (both, both, both, both, both, last, last, last, rows, rows, rows, rows)
    return jax.shard_map(body, mesh=mesh, in_specs=placed, out_specs=both, check_vma=False)
```

time: 774 us -> 102 us (0.13)
  waiting for transfers between devices: 652 us -> 0 us
  Pallas kernels: 0 us -> 100 us
  local copies, waits for them, and re-layouts: 34.9 us -> 1.67 us
  matrix products: 29.8 us -> 0 us
  starting transfers between devices: 23.6 us -> 0 us
  other arithmetic: 19.4 us -> 0 us
  between operations: 13.4 us -> 0.01 us
    all_gather x3 -> x0, waiting for transfers between devices: 465 us -> none  [the longest x1 287 us: body(): lax.all_gather(dense_up, 'expert', axis=0, tiled=True)]
    all_to_all x2 -> x0, waiting for transfers between devices: 109 us -> none  [the longest x1 109 us: body(): lax.all_to_all(pack_slots(whole_rows, flat_slot, groups * capacity, group...]
    pallas_call x0 -> x1, Pallas kernels: none -> 100 us  [run_kernel(): pl.pallas_call(kernel, out_shape=jax.ShapeDtypeStruct((n_tok, dq), BF16),...]
    reduce_scatter x1 -> x0, waiting for transfers between devices: 75.9 us -> none  [body(): lax.psum_scatter(together.astype(jnp.bfloat16), 'tensor', scatter_dimensi...]
    dot_general x7 -> x0, matrix products: 29.8 us -> none  [the longest x2 8.98 us: project_back(): jnp.einsum('tf,df->td', gate_back, gate_matrix, preferred_element_type=jn...]
    all_to_all x2 -> x0, starting transfers between devices: 23 us -> none  [the longest x1 12.6 us: body(): lax.all_to_all(expert_part.reshape(groups, capacity, expert_part.shape[1]...]
    gather x2 -> x0, local copies, waits for them, and re-layouts: 14.1 us -> none  [combine(): picked = buffer[jnp.minimum(flat_slot, buffer.shape[0] - 1)]]
    reshape x5 -> x0, local copies, waits for them, and re-layouts: 14 us -> none  [the longest x1 5.34 us: combine(): buffer = returned.reshape(-1, returned.shape[-1])]
  transfers between devices with their start and end apart: 6 -> 0, of which waited for: 5 -> 0; matrix products, arithmetic and copies ran while one was open for 6% -> 0% of each run, Pallas kernels for 0% -> 0%
where the time goes in v2:
time: 102 us
  Pallas kernels  100 us (98%)
  local copies, waits for them, and re-layouts  1.67 us (2%)
    pallas_call x1, Pallas kernels, run_kernel(): pl.pallas_call(kernel, out_shape=jax.ShapeDtypeStruct((n_tok, dq), BF16),...  100 us

profile of v2, /device:TPU:1, one launch (start us, length us, event | category | flops | bytes accessed | tf_op | source)
XLA Modules:
  0.0 102.1 jit_solution(6818728036473207008)
XLA Ops:
  0.0 100.4 %shard_map.136 = bf16[128,1024]{1,0:T(8,128)(2,1)} custom-call(bf16[128,1024]{1,0:T(8,128)(2,1)} %tok.1, s32[2,128]{1,0:T(2,128)} %bitcast.10, s32[2,128]{1,0:T(2,128)} %bitcast.11, s32[2,128]{1,0:T(2,128)} %bitcast.12, f32[2,128]{1,0:T(2,128)} %bitcast.13, bf16[64,640]{1,0:T(8,128)(2,1)} %dg.1, bf16[64,640]{1,0:T(8,128)(2,1)} %du.1, bf16[128,640]{1,0:T(8,128)(2,1)} %dh.1, ...), custom_call_target="tpu_custom_call" | custom-call | tf_op jit(solution)/shard_map/pallas_call | solution.py:445
  100.4 1.7 %copy.16 = bf16[128,1024]{1,0:T(8,128)(2,1)} copy(bf16[128,1024]{1,0:T(8,128)(2,1)} %shard_map.136) | data formatting | bytes 524288

commit v3 on v2

--- a/solution.py
+++ b/solution.py
@@ -13,7 +13,7 @@
 
 X, Z = 4, 8
 CAP = 5
-CHUNKS = 2
+CHUNKS = 4
 
 
 def sizes():
@@ -226,12 +226,14 @@
             b_fwd[s - 1].wait_recv()
             if s < fwd_steps:
                 zz = zr(-s)
-                b_fwd.append(push(Wd.at[1, :, zz], Wd.at[1, :, zz], z_next))
-            if s <= bwd_steps:
+                some = pl.ds(0, X // 2 if s == bwd_steps else X)
+                b_fwd.append(push(Wd.at[1, some, zz], Wd.at[1, some, zz], z_next))
+            if len(b_bwd) >= s:
                 b_bwd[s - 1].wait_recv()
-                if s < bwd_steps:
-                    zz = zr(s)
-                    b_bwd.append(push(Wd.at[1, :, zz], Wd.at[1, :, zz], z_prev))
+            if s < fwd_steps:
+                zz = zr(s)
+                some = pl.ds(X // 2, X - X // 2) if s == bwd_steps else pl.ds(0, X)
+                b_bwd.append(push(Wd.at[1, some, zz], Wd.at[1, some, zz], z_prev))
         return run
 
     ag_tasks = [ag_start, b_start]
@@ -374,10 +376,6 @@
             if not dyh:
                 Dtot[...] = total
 
-    if DENSE == 0:
-        dense_forward()
-        dense_back()
-
     z_back = []
     for h in range(CHUNKS):
         for dyl, dyh in others:
@@ -387,13 +385,9 @@
         Z2[h] = dot(perms[2], stack(R2[h].reshape(slots, dc))).astype(BF16).reshape(Z, 2 * X * ten, w)
         z_back.append([push(Z2.at[h, zr(d)], ZB.at[h, z], dev(yl, x, zr(d), yh, c)) for d in z_order])
         ZB[h, z] = Z2[h, z]
-        if DENSE == 1 and h == 0:
+        if h == CHUNKS // 2 - 1:
             dense_forward()
-    if DENSE == 1:
-        dense_back()
-    if DENSE == 2:
-        dense_forward()
-        dense_back()
+            dense_back()
     x_back = []
     for h in range(CHUNKS):
         for copy in z_back[h]:
@@ -422,8 +416,7 @@
         copy.wait_send()
 
 
-SERVICE = {"x1": 1, "z1": 1, "y0": 1, "f0": 1, "y1": 1, "f1": 2, "b0": 2, "b1": 1}
-DENSE = 1
+SERVICE = {"x3": 1, "t": 1, "z0": 1, "z3": 1, "y0": 1, "f2": 1, "y3": 1, "f3": 2, "b1": 1}
 N_SEMS = 256
 
 

time: 102 us -> 102 us (level)
  no operation moved by 1% of the time
where the time goes in v3:
time: 102 us
  Pallas kernels  100 us (98%)
  local copies, waits for them, and re-layouts  1.67 us (2%)
    pallas_call x1, Pallas kernels, run_kernel(): pl.pallas_call(kernel, out_shape=jax.ShapeDtypeStruct((n_tok, dq), BF16),...  100 us

profile of v3, /device:TPU:1, one launch (start us, length us, event | category | flops | bytes accessed | tf_op | source)
XLA Modules:
  0.0 102.1 jit_solution(14517314732711013035)
XLA Ops:
  0.0 100.4 %shard_map.136 = bf16[128,1024]{1,0:T(8,128)(2,1)} custom-call(bf16[128,1024]{1,0:T(8,128)(2,1)} %tok.1, s32[2,128]{1,0:T(2,128)} %bitcast.10, s32[2,128]{1,0:T(2,128)} %bitcast.11, s32[2,128]{1,0:T(2,128)} %bitcast.12, f32[2,128]{1,0:T(2,128)} %bitcast.13, bf16[64,640]{1,0:T(8,128)(2,1)} %dg.1, bf16[64,640]{1,0:T(8,128)(2,1)} %du.1, bf16[128,640]{1,0:T(8,128)(2,1)} %dh.1, ...), custom_call_target="tpu_custom_call" | custom-call | tf_op jit(solution)/shard_map/pallas_call | solution.py:438
  100.4 1.7 %copy.16 = bf16[128,1024]{1,0:T(8,128)(2,1)} copy(bf16[128,1024]{1,0:T(8,128)(2,1)} %shard_map.136) | data formatting | bytes 524288

commit v4 on v3

--- a/solution.py
+++ b/solution.py
@@ -197,7 +197,6 @@
         a_fwd.append(push(Wd.at[0, x, z], Wd.at[0, x, z], z_next))
         if bwd_steps:
             a_bwd.append(push(Wd.at[0, x, z], Wd.at[0, x, z], z_prev))
-        a_spread(z)
 
     def b_start():
         for copy in b_x:
@@ -205,6 +204,7 @@
         b_fwd.append(push(Wd.at[1, :, z], Wd.at[1, :, z], z_next))
         if bwd_steps:
             b_bwd.append(push(Wd.at[1, :, z], Wd.at[1, :, z], z_prev))
+        a_spread(z)
 
     def a_step(s):
         def run():
@@ -260,11 +260,6 @@
         B2[h, z] = B1p[h, z]
         service(f"x{h}")
 
-    for (dyl, dyh), copy in zip(others, t_first):
-        copy.wait_recv()
-        yl_, yh_ = chip(dyl, dyh)
-        held = T.at[yl_, :, lanes(yh_ * 2 + c, dq)]
-        t_sib.append(push(held, held, sibling))
     build_order(2)
     build_order(3)
     service("t")
@@ -283,6 +278,12 @@
         y_sib.append([push(B2p.at[h, yl], here, sibling)])
         Xe[h, yl, :, lanes(t, dc)] = B2p[h, yl]
         service(f"z{h}")
+
+    for (dyl, dyh), copy in zip(others, t_first):
+        copy.wait_recv()
+        yl_, yh_ = chip(dyl, dyh)
+        held = T.at[yl_, :, lanes(yh_ * 2 + c, dq)]
+        t_sib.append(push(held, held, sibling))
 
     for h in range(CHUNKS):
         for i in (1, 2, 0):
@@ -416,7 +417,7 @@
         copy.wait_send()
 
 
-SERVICE = {"x3": 1, "t": 1, "z0": 1, "z3": 1, "y0": 1, "f2": 1, "y3": 1, "f3": 2, "b1": 1}
+SERVICE = {"x3": 1, "z1": 1, "z3": 1, "f0": 1, "y1": 1, "f2": 1, "y3": 1, "f3": 1, "b0": 1, "b1": 1}
 N_SEMS = 256
 
 

time: 102 us -> 100 us (0.980)
  Pallas kernels: 100 us -> 98.2 us
    pallas_call x1, Pallas kernels: 100 us -> 98.2 us  [run_kernel(): pl.pallas_call(kernel, out_shape=jax.ShapeDtypeStruct((n_tok, dq), BF16),...]
where the time goes in v4:
time: 100 us; the launch traced here: 99.9 us
  Pallas kernels  98.2 us (98%)
  local copies, waits for them, and re-layouts  1.67 us (2%)
    pallas_call x1, Pallas kernels, run_kernel(): pl.pallas_call(kernel, out_shape=jax.ShapeDtypeStruct((n_tok, dq), BF16),...  98.2 us

profile of v4, /device:TPU:1, one launch (start us, length us, event | category | flops | bytes accessed | tf_op | source)
XLA Modules:
  0.0 99.9 jit_solution(277757370721759942)
XLA Ops:
  0.0 98.2 %shard_map.136 = bf16[128,1024]{1,0:T(8,128)(2,1)} custom-call(bf16[128,1024]{1,0:T(8,128)(2,1)} %tok.1, s32[2,128]{1,0:T(2,128)} %bitcast.10, s32[2,128]{1,0:T(2,128)} %bitcast.11, s32[2,128]{1,0:T(2,128)} %bitcast.12, f32[2,128]{1,0:T(2,128)} %bitcast.13, bf16[64,640]{1,0:T(8,128)(2,1)} %dg.1, bf16[64,640]{1,0:T(8,128)(2,1)} %du.1, bf16[128,640]{1,0:T(8,128)(2,1)} %dh.1, ...), custom_call_target="tpu_custom_call" | custom-call | tf_op jit(solution)/shard_map/pallas_call | solution.py:439
  98.2 1.7 %copy.16 = bf16[128,1024]{1,0:T(8,128)(2,1)} copy(bf16[128,1024]{1,0:T(8,128)(2,1)} %shard_map.136) | data formatting | bytes 524288
